TPU v7x, 128 devices: a whole 4x4x4 slice. The times are simulated.
128 devices in a mesh: blk: 32 (over x, z, y_lo), dp: 4 (over y_hi, core).
Axes of the slice: x: 4, y: 4 (y_hi: 2, y_lo: 2; y = y_hi * 2 + y_lo), z: 4, core: 2. Of those that a mesh axis runs over, the one named last changes fastest.
Arguments:
- embeddings: bfloat16 [32768, 512], P(('dp', 'blk')), may hold values from -16 to 16
- centers: bfloat16 [65536, 512], P(('blk', 'dp')), may hold values from -10 to 10
- labels: int32 [32768], P(('dp', 'blk')), may hold values from 0 to 65535
Outputs:
- loss: float32 [32768], P(('dp', 'blk'))
All inputs are finite; a program needn't handle non-finite values.
Results may differ from a plain program's by a relative error of at most 0.0017.
Values may be sent and summed in bfloat16 or wider, within the bound.
No kernel may reach another device: no remote copies, remote signals or barrier semaphores. Data moves between devices by JAX's collectives and lax.ppermute only.
A program may use at most 128 MiB of HBM per device.

v0:
```python
import math
import jax
import jax.numpy as jnp
from jax import lax
from jax.sharding import Mesh
from jax.sharding import PartitionSpec as P

BLK = ("blk_0", "blk_1", "blk_2")
DP_BLK = ("dp", "blk_0", "blk_1", "blk_2")
BLK_DP = ("blk_0", "blk_1", "blk_2", "dp")
EPSILON = 1e-06
LOGIT_SCALE = 30.0
MARGIN = 0.5


def laid_out(tiles, dim):
    lengths = list(tiles.shape[1:])
    lengths[dim] *= tiles.shape[0]
    return jnp.moveaxis(tiles, 0, dim).reshape(lengths)


def sent_to_all(x, axis):
    length = lax.axis_size(axis)
    return lax.all_to_all(jnp.broadcast_to(x[None], (length, *x.shape)), axis, 0, 0, tiled=True)


def collect(x, axis, dim):
    return laid_out(sent_to_all(x, axis), dim)


def gather_in_order(x, axes, order):
    tiles = x[None]
    for k in order:
        tiles = lax.all_gather(tiles, axes[k], axis=0, tiled=True)
    carried = [lax.axis_size(axes[k]) for k in reversed(order)]
    tiles = tiles.reshape(*carried, *x.shape)
    turned = sorted(range(len(order)), key=lambda place: order[len(order) - 1 - place])
    return tiles.transpose(*turned, *range(len(order), tiles.ndim)).reshape(-1, *x.shape)


def gather_axes(x, axes, order, dim):
    return laid_out(gather_in_order(x, axes, order), dim)


def split_up(x, dim, length):
    before, after = (x.shape[:dim], x.shape[dim + 1 :])
    return jnp.moveaxis(x.reshape(*before, length, -1, *after), dim, 0)


def sum_at_owner(x, axis, dim):
    length = lax.axis_size(axis)
    tiles = lax.all_to_all(split_up(x, dim, length), axis, 0, 0, tiled=True)
    return jnp.sum(tiles, axis=0)


def unit_rows(matrix):
    values = matrix.astype(jnp.float32)
    return (values * lax.rsqrt(jnp.sum(values * values, axis=1, keepdims=True) + EPSILON)).astype(
        jnp.bfloat16
    )


def margin_loss(other_sum, target_cos):
    sine = jnp.sqrt(jnp.maximum(1.0 - target_cos * target_cos, 0.0))
    shifted = target_cos * math.cos(MARGIN) - sine * math.sin(MARGIN)
    return (
        LOGIT_SCALE
        + jnp.log(other_sum + jnp.exp(LOGIT_SCALE * shifted - LOGIT_SCALE))
        - LOGIT_SCALE * shifted
    )


def block_terms(rows, row_labels, centers_block, class_start):
    cosine = jnp.einsum("nd,cd->nc", rows, centers_block, preferred_element_type=jnp.float32)
    columns = class_start + jnp.arange(centers_block.shape[0], dtype=jnp.int32)
    is_target = row_labels[:, None] == columns[None, :]
    other_sum = jnp.sum(
        jnp.where(is_target, 0.0, jnp.exp(LOGIT_SCALE * cosine - LOGIT_SCALE)), axis=1
    )
    target_cos = jnp.sum(jnp.where(is_target, cosine, 0.0), axis=1)
    return (other_sum, target_cos)


def body(embeddings, centers, labels):
    emb_unit = unit_rows(embeddings)
    center_unit = unit_rows(centers)
    shard_classes = center_unit.shape[0]
    group_count = lax.axis_size("dp")
    group_index = lax.axis_index("dp")
    group_rows, group_labels = (collect(emb_unit, "dp", 0), collect(labels, "dp", 0))
    group_total = group_rows.shape[0]
    zeros_sum = jnp.zeros((group_total,), jnp.float32)
    pieces = gather_axes(center_unit, BLK, (2, 0, 1), 0)
    span_rows = math.gcd(math.gcd(pieces.shape[0], shard_classes), 512)

    def one_span(accum, step_index):
        first = step_index * span_rows
        block_rows = lax.dynamic_slice_in_dim(pieces, step_index * span_rows, span_rows, 0)
        class_start = (
            first // shard_classes * group_count + group_index
        ) * shard_classes + first % shard_classes
        other_part, target_part = block_terms(group_rows, group_labels, block_rows, class_start)
        return ((accum[0] + other_part, accum[1] + target_part), None)

    result, ignored = lax.scan(
        one_span, (zeros_sum, zeros_sum), jnp.arange(pieces.shape[0] // span_rows, dtype=jnp.int32)
    )
    other_group, target_group = result
    other_sum, target_cos = (
        sum_at_owner(other_group, "dp", 0),
        sum_at_owner(target_group, "dp", 0),
    )
    return margin_loss(other_sum, target_cos)


def solution(mesh):
    finer = Mesh(mesh.devices.reshape(4, 4, 2, mesh.shape["dp"]), ("blk_0", "blk_1", "blk_2", "dp"))
    placed = (P(DP_BLK, None), P(BLK_DP, None), P(DP_BLK))
    return jax.shard_map(body, mesh=finer, in_specs=placed, out_specs=P(DP_BLK), check_vma=False)
```

profile of v0, /device:TPU:1, one launch (start us, length us, event | category | flops | bytes accessed | tf_op | source)
XLA Modules:
  0.0 432.8 jit_solution(17319401200410657807)
XLA Ops:
  7.8 2.0 fusion.8
  9.8 27.1 %all-gather.9.cloned.1.call-done = bf16[1024,512]{1,0:T(8,128)(2,1)} async-done(((bf16[512,512]{1,0:T(8,128)(2,1)}), bf16[1024,512]{1,0:T(8,128)(2,1)}) %all-gather.9.cloned.1.call-update) | async-done | bytes 1048592 | tf_op jit(solution)/shard_map/all_gather | solution.py:34
  37.1 50.8 %all-gather.5.cloned.1.call-done = bf16[8,512,512]{2,1,0:T(8,128)(2,1)} async-done(((bf16[2,512,512]{2,1,0:T(8,128)(2,1)}), bf16[8,512,512]{2,1,0:T(8,128)(2,1)}) %all-gather.5.cloned.1.call-update) | async-done | bytes 4194320 | tf_op jit(solution)/shard_map/all_gather | solution.py:34
  89.2 5.0 %all-to-all-start = ((s32[4,1,256]{2,1,0:T(1,128)}), s32[4,1,256]{2,1,0:T(1,128)S(1)}, u32[]{:S(2)}, u32[]{:S(2)}) async-start(s32[4,1,256]{2,1,0:T(1,128)} %broadcast_in_dim.31), calls=%async_computation | async-start | bytes 8192 | tf_op jit(solution)/shard_map/all_to_all | solution.py:24
  94.4 4.3 %all-to-all-done = s32[4,1,256]{2,1,0:T(1,128)S(1)} async-done(((s32[4,1,256]{2,1,0:T(1,128)}), s32[4,1,256]{2,1,0:T(1,128)S(1)}, u32[]{:S(2)}, u32[]{:S(2)}) %all-to-all-start) | async-done | bytes 4128 | tf_op jit(solution)/shard_map/all_to_all | solution.py:24
  99.8 4.2 all-to-all-start.1
  104.0 140.1 %all-gather.7.cloned.1.call-done = bf16[32,512,512]{2,1,0:T(8,128)(2,1)} async-done(((bf16[8,512,512]{2,1,0:T(8,128)(2,1)}), bf16[32,512,512]{2,1,0:T(8,128)(2,1)}) %all-gather.7.cloned.1.call-update) | async-done | bytes 16777232 | tf_op jit(solution)/shard_map/all_gather | solution.py:34
  244.1 13.7 %copy.7 = bf16[4,4,2,512,512]{4,3,2,1,0:T(8,128)(2,1)} copy(bf16[4,4,2,512,512]{4,3,2,0,1:T(8,128)(2,1)} %bitcast.35) | data formatting | bytes 33554432 | tf_op jit(solution)/shard_map/transpose | solution.py:38
  257.9 150.0 %while.15 = (s32[]{:T(128)}, f32[1024]{0:T(1024)S(1)}, f32[1024]{0:T(1024)}, s32[4,256]{1,0:T(4,128)S(1)}, s32[32]{0:T(128)S(1)}, /*index=5*/s32[]{:T(128)}, bf1...) while((s32[]{:T(128)}, f32[1024]{0:T(1024)S(1)}, ...), condition=%wide.region_5.6_spmd.clone, body=%wide.region_2.5_spmd.clone.sunk | while | flops 540543488 | bytes 1622475 | solution.py:105
  259.2 2.1 fusion.15
  263.2 2.1 fusion.15
  267.9 2.1 fusion.15
  270.0 1.3 select_add_fusion.3
  272.6 2.1 fusion.15
  274.7 1.3 select_add_fusion.3
  277.3 2.1 fusion.15
  279.4 1.3 select_add_fusion.3
  282.0 2.1 fusion.15
  284.2 1.3 select_add_fusion.3
  286.7 2.1 fusion.15
  291.5 2.1 fusion.15
  293.6 1.3 select_add_fusion.3
  296.2 2.1 fusion.15
  298.3 1.3 select_add_fusion.3
  300.9 2.1 fusion.15
  303.0 1.3 select_add_fusion.3
  305.6 2.1 fusion.15
  307.7 1.3 select_add_fusion.3
  310.3 2.1 fusion.15
  312.4 1.3 select_add_fusion.3
  315.0 2.1 fusion.15
  317.1 1.3 select_add_fusion.3
  319.7 2.1 fusion.15
  324.4 2.1 fusion.15
  326.5 1.3 select_add_fusion.3
  329.1 2.1 fusion.15
  331.2 1.3 select_add_fusion.3
  333.8 2.1 fusion.15
  335.9 1.3 select_add_fusion.3
  338.5 2.1 fusion.15
  340.6 1.3 select_add_fusion.3
  343.2 2.1 fusion.15
  347.9 2.1 fusion.15
  350.1 1.3 select_add_fusion.3
  352.7 2.1 fusion.15
  354.8 1.3 select_add_fusion.3
  357.4 2.1 fusion.15
  359.5 1.3 select_add_fusion.3
  362.1 2.1 fusion.15
  364.2 1.3 select_add_fusion.3
  366.8 2.1 fusion.15
  368.9 1.3 select_add_fusion.3
  371.5 2.1 fusion.15
  373.6 1.3 select_add_fusion.3
  376.2 2.1 fusion.15
  380.9 2.1 fusion.15
  385.6 2.1 fusion.15
  390.3 2.1 fusion.15
  395.0 2.1 fusion.15
  399.7 2.1 fusion.15
  404.4 2.1 fusion.15
  407.8 9.3 %all_to_all.32 = f32[4,1,256]{2,1,0:T(1,128)S(1)} all-to-all(f32[4,1,256]{2,1,0:T(1,128)S(1)} %bitcast.38), channel_id=1, replica_groups=mesh['blk_0'=4,'blk_1'=4,'blk_2'=2,'dp'=4] {'dp'}, dimensions={0} | all-to-all | bytes 8192 | tf_op jit(solution)/shard_map/all_to_all | solution.py:52
  417.2 3.9 all-to-all-start.3
  421.0 4.6 %all-to-all-done.3 = f32[4,1,256]{2,1,0:T(1,128)S(1)} async-done(((f32[4,1,256]{2,1,0:T(1,128)}), f32[4,1,256]{2,1,0:T(1,128)S(1)}, u32[]{:S(2)}, u32[]{:S(2)}) %all-to-all-start.3) | async-done | bytes 4128 | tf_op jit(solution)/shard_map/all_to_all | solution.py:52
  (133 shorter events, 38.9 us)
Async XLA Ops:
  6.5 30.5 %all-gather.9.cloned.1.call-start = ((), (), s32[]{:S(2)}) async-start(), calls=%async_computation.6 | async-start | bytes 1572864 | tf_op jit(solution)/shard_map/all_gather | solution.py:34
  9.8 78.1 %all-gather.5.cloned.1.call-start = ((), (), s32[]{:S(2)}) async-start(), calls=%async_computation.4 | async-start | bytes 5242880 | tf_op jit(solution)/shard_map/all_gather | solution.py:34
  37.0 207.1 %all-gather.7.cloned.1.call-start = ((), (), s32[]{:S(2)}) async-start(), calls=%async_computation.5 | async-start | bytes 20971520 | tf_op jit(solution)/shard_map/all_gather | solution.py:34
  87.9 0.7 copy-start.1
  87.9 6.2 %copy-start = (bf16[256,512]{1,0:T(8,128)(2,1)S(1)}, bf16[256,512]{1,0:T(8,128)(2,1)}, u32[]{:S(2)}) copy-start(bf16[256,512]{1,0:T(8,128)(2,1)} %param.5) | copy-start | bytes 786436
  89.2 9.5 %all-to-all-start = ((s32[4,1,256]{2,1,0:T(1,128)}), s32[4,1,256]{2,1,0:T(1,128)S(1)}, u32[]{:S(2)}, u32[]{:S(2)}) async-start(s32[4,1,256]{2,1,0:T(1,128)} %broadcast_in_dim.31), calls=%async_computation | async-start | bytes 8192 | tf_op jit(solution)/shard_map/all_to_all | solution.py:24
  99.8 158.1 %all-to-all-start.1 = ((bf16[4,256,512]{2,1,0:T(8,128)(2,1)}), bf16[4,256,512]{2,1,0:T(8,128)(2,1)S(1)}, u32[]{:S(2)}, u32[]{:S(2)}) async-start(bf16[4,256,512]{2,1,0:T(8,128)(2,1)} %broadcast_in_dim.33), calls=%async_computation.1 | async-start | bytes 2097152 | tf_op jit(solution)/shard_map/all_to_all | solution.py:24
  417.2 8.4 %all-to-all-start.3 = ((f32[4,1,256]{2,1,0:T(1,128)}), f32[4,1,256]{2,1,0:T(1,128)S(1)}, u32[]{:S(2)}, u32[]{:S(2)}) async-start(f32[4,1,256]{2,1,0:T(1,128)} %bitcast.6), calls=%async_computation.3 | async-start | bytes 8192 | tf_op jit(solution)/shard_map/all_to_all | solution.py:52
Sparse Core Ops, SparseCore 0:
  9.9 27.0 all-gather.8
  38.7 49.1 all-gather.4
  89.6 154.4 all-gather.6
where the time goes:
time: 436 us; the launch traced here: 433 us
  waiting for transfers between devices  227 us (52%)
  matrix products  67.3 us (15%)
  other arithmetic  44.4 us (10%)
  local copies, waits for them, and re-layouts  35.7 us (8%)
  loops' own time  22.9 us (5%)
  starting transfers between devices  13.1 us (3%)
  between operations  13.1 us (3%)
  blocking collectives  9.34 us (2%)
    all_gather x3, waiting for transfers between devices, gather_in_order(): tiles = lax.all_gather(tiles, axes[k], axis=0, tiled=True)  218 us
    dot_general x32, matrix products, block_terms(): jnp.einsum('nd,cd->nc', rows, centers_block, preferred_element_type=jnp.f...  67.3 us
    add x32, other arithmetic, one_span(): return ((accum[0] + other_part, accum[1] + target_part), None)  40.1 us
    another operation x1, loops' own time, body(): lax.scan(one_span, (zeros_sum, zeros_sum), jnp.arange(pieces.shape[0] //...  22.9 us
    dynamic_slice x32, local copies, waits for them, and re-layouts, body(): lax.scan(one_span, (zeros_sum, zeros_sum), jnp.arange(pieces.shape[0] //...  19.5 us
    transpose x1, local copies, waits for them, and re-layouts, gather_in_order(): tiles.transpose(*turned, *range(len(order), tiles.ndim))  13.7 us
    all_to_all x1, blocking collectives, sum_at_owner(): tiles = lax.all_to_all(split_up(x, dim, length), axis, 0, 0, tiled=True)  9.34 us
    all_to_all x2, starting transfers between devices, sent_to_all(): lax.all_to_all(jnp.broadcast_to(x[None], (length, *x.shape)), axis, 0, 0,...  9.18 us
  transfers between devices with their start and end apart: 6, of which 5 were waited for; matrix products, arithmetic and copies ran while one was open for 4% of the time, Pallas kernels for 0%

commit v1 on v0

--- a/solution.py
+++ b/solution.py
@@ -31,7 +31,9 @@
 def gather_in_order(x, axes, order):
     tiles = x[None]
     for k in order:
-        tiles = lax.all_gather(tiles, axes[k], axis=0, tiled=True)
+        tiles = jnp.concatenate(
+            lax.all_to_all(jnp.stack([tiles] * lax.axis_size(axes[k])), axes[k], 0, 0), axis=0
+        )
     carried = [lax.axis_size(axes[k]) for k in reversed(order)]
     tiles = tiles.reshape(*carried, *x.shape)
     turned = sorted(range(len(order)), key=lambda place: order[len(order) - 1 - place])

time: 436 us -> 463 us (1.062)
  blocking collectives: 9.34 us -> 74.1 us
  waiting for transfers between devices: 227 us -> 190 us
  between operations: 13.1 us -> 0.07 us
  starting transfers between devices: 13.1 us -> 23.9 us
  local copies, waits for them, and re-layouts: 35.7 us -> 40.9 us
    all_gather x3 -> x0, waiting for transfers between devices: 218 us -> none  [gather_in_order(): tiles = lax.all_gather(tiles, axes[k], axis=0, tiled=True)]
    all_to_all x0 -> x1, waiting for transfers between devices: none -> 182 us  [gather_in_order(): lax.all_to_all(jnp.stack([tiles] * lax.axis_size(axes[k])), axes[k], 0, 0)]
    all_to_all x0 -> x2, blocking collectives: none -> 66.2 us  [gather_in_order(): lax.all_to_all(jnp.stack([tiles] * lax.axis_size(axes[k])), axes[k], 0, 0)]
    all_to_all x0 -> x1, starting transfers between devices: none -> 7.09 us  [gather_in_order(): lax.all_to_all(jnp.stack([tiles] * lax.axis_size(axes[k])), axes[k], 0, 0)]
    another operation x0 -> x2, local copies, waits for them, and re-layouts: none -> 6.18 us  [gather_in_order(): jnp.stack([tiles] * lax.axis_size(axes[k]))]
  transfers between devices with their start and end apart: 6 -> 4, of which waited for: 5 -> 4; matrix products, arithmetic and copies ran while one was open for 4% -> 4% of each run, Pallas kernels for 0% -> 0%
where the time goes in v1:
time: 463 us; the launch traced here: 460 us
  waiting for transfers between devices  190 us (41%)
  blocking collectives  74.1 us (16%)
  matrix products  67.2 us (15%)
  other arithmetic  43.5 us (9%)
  local copies, waits for them, and re-layouts  40.9 us (9%)
  starting transfers between devices  23.9 us (5%)
  loops' own time  20.5 us (4%)
    all_to_all x1, waiting for transfers between devices, gather_in_order(): lax.all_to_all(jnp.stack([tiles] * lax.axis_size(axes[k])), axes[k], 0, 0)  182 us
    dot_general x32, matrix products, block_terms(): jnp.einsum('nd,cd->nc', rows, centers_block, preferred_element_type=jnp.f...  67.2 us
    all_to_all x2, blocking collectives, gather_in_order(): lax.all_to_all(jnp.stack([tiles] * lax.axis_size(axes[k])), axes[k], 0, 0)  66.2 us
    add x32, other arithmetic, one_span(): return ((accum[0] + other_part, accum[1] + target_part), None)  39.9 us
    another operation x1, loops' own time, body(): lax.scan(one_span, (zeros_sum, zeros_sum), jnp.arange(pieces.shape[0] //...  20.5 us
    dynamic_slice x32, local copies, waits for them, and re-layouts, body(): lax.scan(one_span, (zeros_sum, zeros_sum), jnp.arange(pieces.shape[0] //...  18.5 us
    transpose x1, local copies, waits for them, and re-layouts, gather_in_order(): tiles.transpose(*turned, *range(len(order), tiles.ndim))  13.8 us
    all_to_all x2, starting transfers between devices, sent_to_all(): lax.all_to_all(jnp.broadcast_to(x[None], (length, *x.shape)), axis, 0, 0,...  13 us
  transfers between devices with their start and end apart: 4, of which 4 were waited for; matrix products, arithmetic and copies ran while one was open for 4% of the time, Pallas kernels for 0%

profile of v1, /device:TPU:1, one launch (start us, length us, event | category | flops | bytes accessed | tf_op | source)
XLA Modules:
  0.0 459.7 jit_solution(13390531870832766287)
XLA Ops:
  0.0 1.3 broadcast_in_dim.28
  1.3 6.0 %all-to-all-start = ((s32[4,1,256]{2,1,0:T(1,128)}), s32[4,1,256]{2,1,0:T(1,128)S(1)}, u32[]{:S(2)}, u32[]{:S(2)}) async-start(s32[4,1,256]{2,1,0:T(1,128)} %broadcast_in_dim.28), calls=%async_computation | async-start | bytes 8192 | tf_op jit(solution)/shard_map/all_to_all | solution.py:24
  9.8 2.1 all-to-all-done
  11.8 15.4 %all_to_all.47 = bf16[2,1,512,512]{3,2,1,0:T(8,128)(2,1)S(1)} all-to-all(bf16[2,1,512,512]{3,2,1,0:T(8,128)(2,1)S(1)} %pad_maximum_fusion), channel_id=1, replica_groups=mesh['blk_0'=4,'blk_1'=4,'blk_2'=2,'dp'=4] {'blk_2'}, dimensions={0} | all-to-all | bytes 2097152 | tf_op jit(solution)/shard_map/all_to_all | solution.py:35
  27.6 50.8 %all_to_all.48 = bf16[4,2,512,512]{3,2,1,0:T(8,128)(2,1)S(1)} all-to-all(bf16[4,2,512,512]{3,2,1,0:T(8,128)(2,1)S(1)} %stack.10), channel_id=1, replica_groups=mesh['blk_0'=4,'blk_1'=4,'blk_2'=2,'dp'=4] {'blk_0'}, dimensions={0} | all-to-all | bytes 8388608 | tf_op jit(solution)/shard_map/all_to_all | solution.py:35
  78.4 5.8 %stack.11 = bf16[4,8,512,512]{3,2,1,0:T(8,128)(2,1)} broadcast(bf16[8,512,512]{2,1,0:T(8,128)(2,1)S(1)} %bitcast.37), dimensions={1,2,3} | broadcast | bytes 20971520 | tf_op jit(solution)/shard_map/stack | solution.py:35
  84.2 7.1 %all-to-all-start.3 = ((bf16[4,8,512,512]{3,2,1,0:T(8,128)(2,1)}), bf16[4,8,512,512]{3,2,1,0:T(8,128)(2,1)}, u32[]{:S(2)}, u32[]{:S(2)}) async-start(bf16[4,8,512,512]{3,2,1,0:T(8,128)(2,1)} %stack.11), calls=%async_computation.3 | async-start | bytes 33554432 | tf_op jit(solution)/shard_map/all_to_all | solution.py:35
  91.6 181.7 %all-to-all-done.3 = bf16[4,8,512,512]{3,2,1,0:T(8,128)(2,1)} async-done(((bf16[4,8,512,512]{3,2,1,0:T(8,128)(2,1)}), bf16[4,8,512,512]{3,2,1,0:T(8,128)(2,1)}, u32[]{:S(2)}, u32[]{:S(2)}) %all-to-all-start.3) | async-done | bytes 16777248 | tf_op jit(solution)/shard_map/all_to_all | solution.py:35
  274.3 7.0 %all-to-all-start.4 = ((bf16[4,256,512]{2,1,0:T(8,128)(2,1)}), bf16[4,256,512]{2,1,0:T(8,128)(2,1)S(1)}, u32[]{:S(2)}, u32[]{:S(2)}) async-start(bf16[4,256,512]{2,1,0:T(8,128)(2,1)} %broadcast_in_dim.29), calls=%async_computation.4 | async-start | bytes 2097152 | tf_op jit(solution)/shard_map/all_to_all | solution.py:24
  281.3 13.8 %copy.7 = bf16[4,4,2,512,512]{4,3,2,1,0:T(8,128)(2,1)} copy(bf16[4,4,2,512,512]{4,3,2,0,1:T(8,128)(2,1)} %bitcast.4) | data formatting | bytes 33554432 | tf_op jit(solution)/shard_map/transpose | solution.py:40
  295.1 1.3 all-to-all-done.4
  296.4 146.3 %while.15 = (s32[]{:T(128)}, f32[1024]{0:T(1024)S(1)}, f32[1024]{0:T(1024)}, s32[4,256]{1,0:T(4,128)S(1)}, s32[32]{0:T(128)S(1)}, /*index=5*/s32[]{:T(128)}, bf1...) while((s32[]{:T(128)}, f32[1024]{0:T(1024)S(1)}, ...), condition=%wide.region_5.6_spmd.clone, body=%wide.region_2.5_spmd.clone.sunk | while | flops 540543488 | bytes 1622475 | solution.py:107
  297.6 2.1 fusion.16
  301.6 2.1 fusion.16
  303.7 1.3 select_add_fusion.3
  306.2 2.1 fusion.16
  308.3 1.3 select_add_fusion.3
  310.8 2.1 fusion.16
  312.9 1.3 select_add_fusion.3
  315.4 2.1 fusion.16
  317.5 1.3 select_add_fusion.3
  319.9 2.1 fusion.16
  322.1 1.3 select_add_fusion.3
  324.5 2.1 fusion.16
  326.6 1.3 select_add_fusion.3
  329.1 2.1 fusion.16
  331.2 1.3 select_add_fusion.3
  333.7 2.1 fusion.16
  335.8 1.3 select_add_fusion.3
  338.3 2.1 fusion.16
  340.4 1.3 select_add_fusion.3
  342.9 2.1 fusion.16
  345.0 1.3 select_add_fusion.3
  347.5 2.1 fusion.16
  352.1 2.1 fusion.16
  356.7 2.1 fusion.16
  361.3 2.1 fusion.16
  365.9 2.1 fusion.16
  370.5 2.1 fusion.16
  372.6 1.3 select_add_fusion.3
  375.1 2.1 fusion.16
  379.7 2.1 fusion.16
  384.3 2.1 fusion.16
  386.4 1.3 select_add_fusion.3
  388.9 2.1 fusion.16
  391.0 1.3 select_add_fusion.3
  393.4 2.1 fusion.16
  398.0 2.1 fusion.16
  402.6 2.1 fusion.16
  404.7 1.3 select_add_fusion.3
  407.2 2.1 fusion.16
  409.3 1.3 select_add_fusion.3
  411.8 2.1 fusion.16
  416.4 2.1 fusion.16
  421.0 2.1 fusion.16
  425.6 2.1 fusion.16
  430.2 2.1 fusion.16
  432.3 1.3 select_add_fusion.3
  434.8 2.1 fusion.16
  436.9 1.3 select_add_fusion.3
  439.4 2.1 fusion.16
  442.8 7.9 %all_to_all.49 = f32[4,1,256]{2,1,0:T(1,128)S(1)} all-to-all(f32[4,1,256]{2,1,0:T(1,128)S(1)} %bitcast.41), channel_id=1, replica_groups=mesh['blk_0'=4,'blk_1'=4,'blk_2'=2,'dp'=4] {'dp'}, dimensions={0} | all-to-all | bytes 8192 | tf_op jit(solution)/shard_map/all_to_all | solution.py:54
  450.6 3.9 all-to-all-start.6
  454.5 4.6 all-to-all-done.6
  (129 shorter events, 41.9 us)
Async XLA Ops:
  1.3 10.6 %all-to-all-start = ((s32[4,1,256]{2,1,0:T(1,128)}), s32[4,1,256]{2,1,0:T(1,128)S(1)}, u32[]{:S(2)}, u32[]{:S(2)}) async-start(s32[4,1,256]{2,1,0:T(1,128)} %broadcast_in_dim.28), calls=%async_computation | async-start | bytes 8192 | tf_op jit(solution)/shard_map/all_to_all | solution.py:24
  84.2 7.1 %copy-start = (bf16[256,512]{1,0:T(8,128)(2,1)S(1)}, bf16[256,512]{1,0:T(8,128)(2,1)}, u32[]{:S(2)}) copy-start(bf16[256,512]{1,0:T(8,128)(2,1)} %param.5) | copy-start | bytes 786436
  84.2 189.0 %all-to-all-start.3 = ((bf16[4,8,512,512]{3,2,1,0:T(8,128)(2,1)}), bf16[4,8,512,512]{3,2,1,0:T(8,128)(2,1)}, u32[]{:S(2)}, u32[]{:S(2)}) async-start(bf16[4,8,512,512]{3,2,1,0:T(8,128)(2,1)} %stack.11), calls=%async_computation.3 | async-start | bytes 33554432 | tf_op jit(solution)/shard_map/all_to_all | solution.py:35
  274.3 22.1 %all-to-all-start.4 = ((bf16[4,256,512]{2,1,0:T(8,128)(2,1)}), bf16[4,256,512]{2,1,0:T(8,128)(2,1)S(1)}, u32[]{:S(2)}, u32[]{:S(2)}) async-start(bf16[4,256,512]{2,1,0:T(8,128)(2,1)} %broadcast_in_dim.29), calls=%async_computation.4 | async-start | bytes 2097152 | tf_op jit(solution)/shard_map/all_to_all | solution.py:24
  450.6 8.5 %all-to-all-start.6 = ((f32[4,1,256]{2,1,0:T(1,128)}), f32[4,1,256]{2,1,0:T(1,128)S(1)}, u32[]{:S(2)}, u32[]{:S(2)}) async-start(f32[4,1,256]{2,1,0:T(1,128)} %bitcast.8), calls=%async_computation.6 | async-start | bytes 8192 | tf_op jit(solution)/shard_map/all_to_all | solution.py:54
